TPU v7x, 128 devices: a whole 4x4x4 slice. The times are simulated.
128 devices in a mesh: mem: 16 (over y_lo, x, core), strip: 8 (over z, y_hi).
Axes of the slice: x: 4, y: 4 (y_hi: 2, y_lo: 2; y = y_hi * 2 + y_lo), z: 4, core: 2. Of those that a mesh axis runs over, the one named last changes fastest.
Arguments:
- state: float32 [256, 3, 65536], P('mem', None, 'strip'), may hold values from -6 to 6
- courant: float32 [65536], P('strip'), may hold values from 0.5 to 0.95
- angle: float32 [65536], P('strip'), may hold values from -0.4 to 0.4
- obs_index: int32 [4096], P('strip'), may hold values from 0 to 8191
- obs_value: float32 [4096], P('strip'), may hold values from -6 to 6
- obs_variance: float32 [4096], P('strip'), may hold values from 0.1 to 1
- perturb: float32 [256, 4096], P(None, 'strip'), may hold values from -4 to 4
Outputs:
- forecast: float32 [256, 3, 65536], P('mem', None, 'strip')
All inputs are finite; a program needn't handle non-finite values.
Results may differ from a plain program's by a relative error of at most 0.00014.
Values sent between devices are 32-bit elements; how exact they have to be, the bound alone decides.
A program may use at most 128 MiB of HBM per device.

v0:
```python
import functools

import jax
import jax.numpy as jnp
from jax import lax
from jax.experimental import pallas as pl
from jax.experimental.pallas import tpu as pltpu
from jax.sharding import PartitionSpec as P

STEPS_BEFORE = 4
STEPS_AFTER = 2
SQUARINGS = 14
CHUNK = 1024
TILE = 128
MESH = pl.DeviceIdType.MESH
HIGH = lax.Precision.HIGHEST


def dot(a, b, dims=((1,), (0,))):
    return lax.dot_general(a, b, (dims, ((), ())), precision=HIGH, preferred_element_type=jnp.float32)


def cosine_sine(angle):
    t = angle * angle
    cosine = 1.0 + t * (-1 / 2 + t * (1 / 24 + t * (-1 / 720 + t * (1 / 40320 - t * (1 / 3628800)))))
    sine = angle * (1.0 + t * (-1 / 6 + t * (1 / 120 + t * (-1 / 5040 + t * (1 / 362880)))))
    return cosine, sine


def advance(fields, coefs, steps):
    h, u, v = fields
    c, cosine, sine = coefs
    last = h.shape[-1] - 1
    for _ in range(steps):
        a = u + h
        b = u - h
        a = a - c * (a - pltpu.roll(a, 1, axis=1))
        b = b + c * (pltpu.roll(b, last, axis=1) - b)
        speed = 0.5 * (a + b)
        h = 0.5 * (a - b)
        u = cosine * speed + sine * v
        v = cosine * v - sine * speed
    return h, u, v


def kernel(
    state, courant, angle, obs_index, obs_value, obs_variance, perturb, out,
    padded, coef, prior, observed, mine, grid, mixed, analysed,
    local_sem, halo_send, halo_recv, coef_send, coef_recv, obs_send, obs_recv,
    in_send, in_recv, out_send, out_recv, edge_send, edge_recv,
):
    members, columns = state.shape[1], state.shape[2]
    peers = grid.shape[1] // members
    width = grid.shape[2]
    count = peers * members
    nobs = mine.shape[1]
    me = lax.axis_index("mem")
    strip = lax.axis_index("strip")
    strips = lax.axis_size("strip")
    right = (strip + 1) % strips
    left = (strip + strips - 1) % strips

    barrier = pltpu.get_barrier_semaphore()

    def greet(r, carry):
        pl.semaphore_signal(barrier, inc=1, device_id={"mem": (me + r) % peers}, device_id_type=MESH)
        return carry

    lax.fori_loop(1, peers, greet, 0)
    for other in (left, right):
        pl.semaphore_signal(barrier, inc=1, device_id={"strip": other}, device_id_type=MESH)

    load = pltpu.make_async_copy(state, padded.at[:, :, pl.ds(TILE, columns)], local_sem)
    load.start()

    def coefficients(k, carry):
        at = pl.ds(pl.multiple_of(k * CHUNK, CHUNK), CHUNK)
        to = pl.ds(pl.multiple_of(TILE + k * CHUNK, TILE), CHUNK)
        cosine, sine = cosine_sine(jnp.broadcast_to(angle[:, at], (8, CHUNK)))
        coef[0, :, to] = jnp.broadcast_to(courant[:, at], (8, CHUNK))
        coef[1, :, to] = cosine
        coef[2, :, to] = sine
        return carry

    lax.fori_loop(0, columns // CHUNK, coefficients, 0)
    load.wait()

    first, last = pl.ds(TILE, TILE), pl.ds(columns, TILE)
    before, after = pl.ds(0, TILE), pl.ds(columns + TILE, TILE)

    def halo(buffer, send, recv):
        return [
            pltpu.make_async_remote_copy(
                buffer.at[:, :, source], buffer.at[:, :, target], send.at[n], recv.at[n],
                device_id={"strip": other}, device_id_type=MESH,
            )
            for n, (source, target, other) in enumerate([(last, before, right), (first, after, left)])
        ]

    pl.semaphore_wait(barrier, peers + 1)
    halos = halo(padded, halo_send, halo_recv) + halo(coef, coef_send, coef_recv)
    for copy in halos:
        copy.start()

    def steps_of(source, target, offset, steps, k):
        window = pl.ds(pl.multiple_of(k * CHUNK, TILE), CHUNK + 2 * TILE)
        to = pl.ds(pl.multiple_of(offset + k * CHUNK, TILE), CHUNK)
        factors = [coef[f, :, window] for f in range(3)]
        for half in range(members // 8):
            rows = pl.ds(half * 8, 8)
            fields = advance([source[f, rows, window] for f in range(3)], factors, steps)
            for f in range(3):
                target[f, rows, to] = fields[f][:, TILE : TILE + CHUNK]

    chunks = columns // CHUNK

    def before_steps(k, carry):
        steps_of(padded, prior, 0, STEPS_BEFORE, k)
        return carry

    lax.fori_loop(1, chunks - 1, before_steps, 0)
    for copy in halos:
        copy.wait()
    before_steps(0, 0)
    before_steps(chunks - 1, 0)

    groups = nobs // TILE
    tiles = [jnp.broadcast_to(obs_index[g : g + 1, :] // TILE, (8, TILE)) for g in range(groups)]
    lanes = [jnp.broadcast_to(obs_index[g : g + 1, :] % TILE, (8, TILE)) for g in range(groups)]

    def pick(t, found):
        at = pl.ds(pl.multiple_of(t * TILE, TILE), TILE)
        news = []
        for half in range(members // 8):
            heights = prior[0, pl.ds(half * 8, 8), at]
            for g in range(groups):
                value = jnp.take_along_axis(heights, lanes[g], axis=1)
                news.append(jnp.where(tiles[g] == t, value, found[half * groups + g]))
        return tuple(news)

    zero = jnp.zeros((8, TILE), jnp.float32)
    found = lax.fori_loop(0, columns // TILE, pick, (zero,) * (groups * members // 8))
    own = pl.ds(pl.multiple_of(me * members, members), members)
    for half in range(members // 8):
        for g in range(groups):
            mine[pl.ds(half * 8, 8), pl.ds(g * TILE, TILE)] = found[half * groups + g]
    observed[own, :] = mine[...]

    def obs_copy(r):
        return pltpu.make_async_remote_copy(
            mine, observed.at[own, :], obs_send.at[r], obs_recv.at[r],
            device_id={"mem": (me + r) % peers}, device_id_type=MESH,
        )

    def in_copy(r):
        peer = (me + r) % peers
        return pltpu.make_async_remote_copy(
            prior.at[:, :, pl.ds(pl.multiple_of(peer * width, width), width)], grid.at[:, own, :],
            in_send.at[r], in_recv.at[r], device_id={"mem": peer}, device_id_type=MESH,
        )

    def each(make, action):
        def body(r, carry):
            action(make(r))
            return carry

        lax.fori_loop(1, peers, body, 0)

    each(obs_copy, lambda copy: copy.start())
    each(in_copy, lambda copy: copy.start())
    columns_here = pl.ds(pl.multiple_of(me * width, width), width)
    grid[:, own, :] = prior[:, :, columns_here]
    each(obs_copy, lambda copy: copy.wait())

    predicted = observed[...]
    spread = predicted - jnp.sum(predicted, axis=0, keepdims=True) * (1.0 / count)
    innovation = obs_value[...] + perturb[...] - predicted
    scaled = spread / obs_variance[...]
    rows_id = lax.broadcasted_iota(jnp.int32, (count, count), 0)
    cols_id = lax.broadcasted_iota(jnp.int32, (count, count), 1)
    unit = jnp.where(rows_id == cols_id, 1.0, 0.0).astype(jnp.float32)
    low = float(count - 1)
    inner = dot(scaled, spread, ((1,), (1,))) + low * unit
    update = dot(innovation, scaled, ((1,), (1,)))
    high = jnp.max(jnp.sum(jnp.abs(inner), axis=0, keepdims=True), axis=1, keepdims=True)
    rate = 2.0 / (high + low)
    gap = 2.0 * low / (high + low)
    remainder = unit - rate * inner
    update = rate * update
    for n in range(SQUARINGS):
        both = dot(jnp.concatenate([remainder, update], axis=0), remainder)
        shrink = gap * (2.0 - gap)
        scale = 2.0 / (1.0 + shrink)
        gap = scale * shrink
        remainder = scale * both[:count] + (1.0 - scale) * unit
        update = scale * (update + both[count:])
    update = update + dot(update, remainder)

    each(in_copy, lambda copy: copy.wait())

    def out_copy(f, r):
        peer = (me + r) % peers
        return pltpu.make_async_remote_copy(
            mixed.at[f, pl.ds(pl.multiple_of(peer * members, members), members), :],
            analysed.at[f, :, pl.ds(pl.multiple_of(TILE + me * width, TILE), width)],
            out_send.at[f, r], out_recv.at[f, r], device_id={"mem": peer}, device_id_type=MESH,
        )

    for f in range(3):
        block = grid[f]
        mixed[f] = block + dot(update, block)
        each(functools.partial(out_copy, f), lambda copy: copy.start())
    analysed[:, :, pl.ds(pl.multiple_of(TILE + me * width, TILE), width)] = mixed[:, own, :]
    for f in range(3):
        each(functools.partial(out_copy, f), lambda copy: copy.wait())

    edges = halo(analysed, edge_send, edge_recv)
    for copy in edges:
        copy.start()

    def after_steps(k, carry):
        steps_of(analysed, out, 0, STEPS_AFTER, k)
        return carry

    lax.fori_loop(1, chunks - 1, after_steps, 0)
    for copy in edges:
        copy.wait()
    after_steps(0, 0)
    after_steps(chunks - 1, 0)


def local(state, courant, angle, obs_index, obs_value, obs_variance, perturb):
    members, fields, columns = state.shape
    nobs = obs_index.shape[0]
    peers = lax.axis_size("mem")
    count, width = peers * members, columns // peers
    wide = columns + 2 * TILE
    vmem = pl.BlockSpec(memory_space=pltpu.VMEM)
    f32 = jnp.float32
    dma = pltpu.SemaphoreType.DMA
    result = pl.pallas_call(
        kernel,
        out_shape=jax.ShapeDtypeStruct((fields, members, columns), f32),
        in_specs=[pl.BlockSpec(memory_space=pl.ANY)] + [vmem] * 6,
        out_specs=vmem,
        scratch_shapes=[
            pltpu.VMEM((fields, members, wide), f32),
            pltpu.VMEM((3, 8, wide), f32),
            pltpu.VMEM((fields, members, columns), f32),
            pltpu.VMEM((count, nobs), f32),
            pltpu.VMEM((members, nobs), f32),
            pltpu.VMEM((fields, count, width), f32),
            pltpu.VMEM((fields, count, width), f32),
            pltpu.VMEM((fields, members, wide), f32),
            dma,
            dma((2,)), dma((2,)), dma((2,)), dma((2,)),
            dma((peers,)), dma((peers,)), dma((peers,)), dma((peers,)),
            dma((fields, peers)), dma((fields, peers)), dma((2,)), dma((2,)),
        ],
        compiler_params=pltpu.CompilerParams(collective_id=0, has_side_effects=True, vmem_limit_bytes=48 * 2**20),
    )(
        jnp.transpose(state, (1, 0, 2)), courant[None, :], angle[None, :],
        obs_index.reshape(nobs // TILE, TILE), obs_value[None, :], obs_variance[None, :], perturb,
    )
    return jnp.transpose(result, (1, 0, 2))


def solution(mesh):
    in_specs = (
        P("mem", None, "strip"),
        P("strip"),
        P("strip"),
        P("strip"),
        P("strip"),
        P("strip"),
        P(None, "strip"),
    )
    out_specs = P("mem", None, "strip")
    return jax.shard_map(local, mesh=mesh, in_specs=in_specs, out_specs=out_specs, check_vma=False)
```

profile of v0, /device:TPU:1, one launch (start us, length us, event | category | flops | bytes accessed | tf_op | source)
XLA Modules:
  0.0 78.1 jit_solution(17880980002595638042)
XLA Ops:
  0.0 0.0 copy-start
  0.0 1.4 %copy-done = f32[16,3,8192]{2,0,1:T(8,128)S(1)} copy-done((f32[16,3,8192]{2,0,1:T(8,128)S(1)}, f32[16,3,8192]{2,0,1:T(8,128)}, u32[]{:S(2)}) %copy-start) | copy-done | bytes 1572888
  1.4 0.0 copy-start.1
  1.4 1.0 %copy-done.1 = f32[256,512]{1,0:T(8,128)S(1)} copy-done((f32[256,512]{1,0:T(8,128)S(1)}, f32[256,512]{1,0:T(8,128)}, u32[]{:S(2)}) %copy-start.1) | copy-done | bytes 524312
  2.5 0.0 copy-start.2
  2.5 0.8 copy-done.2
  3.2 0.0 copy-start.3
  3.2 0.8 copy-done.3
  4.0 0.0 copy-start.4
  4.0 0.7 copy-done.4
  4.7 0.0 copy-start.5
  4.7 0.7 copy-done.5
  5.3 0.0 copy-start.6
  5.3 0.7 copy-done.6
  6.0 70.9 %shard_map.73 = f32[3,16,8192]{2,1,0:T(8,128)S(1)} custom-call(f32[3,16,8192]{2,1,0:T(8,128)S(1)} %bitcast.8, f32[1,8192]{1,0:T(1,128)S(1)} %bitcast.9, f32[1,8192]{1,0:T(1,128)S(1)} %bitcast.10, s32[4,128]{1,0:T(4,128)S(1)} %bitcast.11, f32[1,512]{1,0:T(1,128)S(1)} %bitcast.12, f32[1,512]{1,0:T(1,128)S(1)} %bitcast.13, f32[256,512]{1,0:T(8,128)S(1)} %copy-done.1), custom_call_target="tpu_custom_call" | custom-call | tf_op jit(solution)/shard_map/pallas_call | solution.py:241
  76.9 1.1 %copy.9 = f32[16,3,8192]{2,0,1:T(8,128)} copy(f32[16,3,8192]{2,0,1:T(8,128)S(1)} %bitcast.7) | data formatting | bytes 3145728
Async XLA Ops:
  0.0 1.4 %copy-start = (f32[16,3,8192]{2,0,1:T(8,128)S(1)}, f32[16,3,8192]{2,0,1:T(8,128)}, u32[]{:S(2)}) copy-start(f32[16,3,8192]{2,0,1:T(8,128)} %param.7) | copy-start | bytes 4718596
  1.4 1.0 %copy-start.1 = (f32[256,512]{1,0:T(8,128)S(1)}, f32[256,512]{1,0:T(8,128)}, u32[]{:S(2)}) copy-start(f32[256,512]{1,0:T(8,128)} %perturb.1) | copy-start | bytes 1572868
  2.5 0.8 copy-start.2
  3.2 0.8 copy-start.3
  4.0 0.7 copy-start.4
  4.7 0.7 copy-start.5
  5.3 0.7 copy-start.6
where the time goes:
time: 78.4 us; the launch traced here: 78.1 us
  Pallas kernels  70.9 us (90%)
  local copies, waits for them, and re-layouts  7.15 us (9%)
    pallas_call x1, Pallas kernels, local(): pl.pallas_call(kernel, out_shape=jax.ShapeDtypeStruct((fields, members, c...  70.9 us
    unnamed x15, local copies, waits for them, and re-layouts  7.15 us

commit v1 on v0

v1 whole, which is shorter than its diff:
```python
import functools

import jax
import jax.numpy as jnp
from jax import lax
from jax.experimental import pallas as pl
from jax.experimental.pallas import tpu as pltpu
from jax.sharding import PartitionSpec as P

STEPS_BEFORE = 4
STEPS_AFTER = 2
SQUARINGS = 12
EXACT = 5
CHUNK = 1024
TILE = 128
PICKS = 31
MESH = pl.DeviceIdType.MESH
HIGH = lax.Precision.HIGHEST


def dot(a, b, dims=((1,), (0,))):
    return lax.dot_general(a, b, (dims, ((), ())), precision=HIGH, preferred_element_type=jnp.float32)


def dot3(a, b):
    a_hi, b_hi = a.astype(jnp.bfloat16), b.astype(jnp.bfloat16)
    a_lo = (a - a_hi.astype(jnp.float32)).astype(jnp.bfloat16)
    b_lo = (b - b_hi.astype(jnp.float32)).astype(jnp.bfloat16)
    rows = a.shape[0]
    both = jnp.dot(jnp.concatenate([a_hi, a_lo], axis=0), b_hi, preferred_element_type=jnp.float32)
    return both[:rows] + (both[rows:] + jnp.dot(a_hi, b_lo, preferred_element_type=jnp.float32))


def cosine_sine(angle):
    t = angle * angle
    cosine = 1.0 + t * (-1 / 2 + t * (1 / 24 + t * (-1 / 720 + t * (1 / 40320 - t * (1 / 3628800)))))
    sine = angle * (1.0 + t * (-1 / 6 + t * (1 / 120 + t * (-1 / 5040 + t * (1 / 362880)))))
    return cosine, sine


def advance(fields, coefs, steps):
    h, u, v = fields
    c, cosine, sine = coefs
    last = h.shape[-1] - 1
    for _ in range(steps):
        a = u + h
        b = u - h
        a = a - c * (a - pltpu.roll(a, 1, axis=1))
        b = b + c * (pltpu.roll(b, last, axis=1) - b)
        speed = 0.5 * (a + b)
        h = 0.5 * (a - b)
        u = cosine * speed + sine * v
        v = cosine * v - sine * speed
    return h, u, v


def kernel(
    state, courant, angle, obs_index, obs_value, obs_variance, perturb, out,
    fields_in, raw, coef, index, value, variance, noise, prior, observed, grid, mixed, analysed,
    halo_in, halo_raw, halo_out,
    load_sem, state_sem, halo_send, halo_recv, obs_send, obs_recv,
    in_send, in_recv, out_send, out_recv, edge_send, edge_recv,
):
    members, columns = state.shape[1], state.shape[2]
    peers = grid.shape[1] // members
    width = grid.shape[2]
    parts = width // TILE
    count = peers * members
    nobs = observed.shape[1]
    chunks = columns // CHUNK
    halves = members // 8
    me = lax.axis_index("mem")
    strip = lax.axis_index("strip")
    strips = lax.axis_size("strip")
    right = (strip + 1) % strips
    left = (strip + strips - 1) % strips
    first, last = pl.ds(0, TILE), pl.ds(columns - TILE, TILE)
    own = pl.ds(pl.multiple_of(me * members, members), members)

    barrier = pltpu.get_barrier_semaphore()

    def greet(r, carry):
        pl.semaphore_signal(barrier, inc=1, device_id={"mem": (me + r) % peers}, device_id_type=MESH)
        return carry

    lax.fori_loop(1, peers, greet, 0)
    for other in (left, right):
        pl.semaphore_signal(barrier, inc=1, device_id={"strip": other}, device_id_type=MESH)

    pairs = [
        (angle, raw.at[0]), (courant, raw.at[1]), (obs_index, index), (obs_value, value),
        (obs_variance, variance), (perturb, noise),
    ]
    loads = [pltpu.make_async_copy(a, b, load_sem.at[n]) for n, (a, b) in enumerate(pairs)]

    def state_load(k):
        at = pl.ds(k * CHUNK, CHUNK)
        return pltpu.make_async_copy(state.at[:, :, at], fields_in.at[:, :, at], state_sem.at[k])

    for load in loads[:2]:
        load.start()
    for k in range(chunks):
        state_load(k).start()
    for load in loads[2:]:
        load.start()

    pl.semaphore_wait(barrier, peers + 1)

    def to_neighbours(source, target, send, recv):
        return [
            pltpu.make_async_remote_copy(
                source.at[..., at], target.at[side], send.at[side], recv.at[side],
                device_id={"strip": other}, device_id_type=MESH,
            )
            for side, (at, other) in enumerate([(last, right), (first, left)])
        ]

    halos = (
        to_neighbours(state, halo_in, halo_send.at[0], halo_recv.at[0])
        + to_neighbours(angle, halo_raw.at[0], halo_send.at[1], halo_recv.at[1])
        + to_neighbours(courant, halo_raw.at[1], halo_send.at[2], halo_recv.at[2])
    )
    for copy in halos:
        copy.start()

    for load in loads[:2]:
        load.wait()

    def factors_of(turn, speed):
        shape = (8, turn.shape[-1])
        cosine, sine = cosine_sine(jnp.broadcast_to(turn, shape))
        return jnp.broadcast_to(speed, shape), cosine, sine

    def coefficients(k, carry):
        at = pl.ds(pl.multiple_of(k * CHUNK, CHUNK), CHUNK)
        for f, factor in enumerate(factors_of(raw[0, :, at], raw[1, :, at])):
            coef[f, :, at] = factor
        return carry

    lax.fori_loop(0, chunks, coefficients, 0)

    def sweep(source, target, steps, k, before=TILE, after=TILE):
        window = pl.ds(pl.multiple_of(k * CHUNK - before, TILE), CHUNK + before + after)
        to = pl.ds(pl.multiple_of(k * CHUNK, CHUNK), CHUNK)
        factors = [coef[f, :, window] for f in range(3)]
        for half in range(halves):
            rows = pl.ds(half * 8, 8)
            news = advance([source[f, rows, window] for f in range(3)], factors, steps)
            for f in range(3):
                target[f, rows, to] = news[f][:, before : before + CHUNK]

    def sweep_all(source, target, steps, ready):
        ready(0)
        ready(1)
        sweep(source, target, steps, 0, before=0)

        def body(k, carry):
            ready(k + 1)
            sweep(source, target, steps, k)
            return carry

        lax.fori_loop(1, chunks - 1, body, 0)
        sweep(source, target, steps, chunks - 1, after=0)

    def sweep_ends(source, halo, target, steps, outer):
        two = [pl.ds(columns - 2 * TILE, 2 * TILE), pl.ds(0, 2 * TILE)]
        for side in range(2):
            inner = two[1 - side]

            def joined(edge, inside, side=side):
                return jnp.concatenate([edge, inside] if side == 0 else [inside, edge], axis=1)

            factors = [joined(outer[side][f], coef[f, :, inner]) for f in range(3)]
            for half in range(halves):
                rows = pl.ds(half * 8, 8)
                window = [joined(halo[side, f, rows, :], source[f, rows, inner]) for f in range(3)]
                news = advance(window, factors, steps)
                for f in range(3):
                    target[f, rows, (first, last)[side]] = news[f][:, TILE : 2 * TILE]

    def state_ready(k):
        at = pl.ds(pl.multiple_of(k * CHUNK, CHUNK), CHUNK)
        pltpu.make_async_copy(state.at[:, :, at], fields_in.at[:, :, at], state_sem.at[k]).wait()

    sweep_all(fields_in, prior, STEPS_BEFORE, state_ready)

    def part_of(peer, q):
        return q + (peer // (peers - 1)) * (parts - 1 - 2 * q)

    def in_copy(q, r):
        peer = (me + r) % peers
        t = part_of(peer, q)
        return pltpu.make_async_remote_copy(
            prior.at[:, :, pl.ds(pl.multiple_of(peer * width + t * TILE, TILE), TILE)],
            grid.at[:, own, pl.ds(pl.multiple_of(t * TILE, TILE), TILE)],
            in_send.at[q, r], in_recv.at[q, r], device_id={"mem": peer}, device_id_type=MESH,
        )

    def each(make, action):
        def body(r, carry):
            action(make(r))
            return carry

        lax.fori_loop(1, peers, body, 0)

    each(functools.partial(in_copy, 1), lambda copy: copy.start())

    for load in loads[2:]:
        load.wait()
    groups = nobs // TILE
    tiles = [jnp.broadcast_to(index[g : g + 1, :] // TILE, (8, TILE)) for g in range(groups)]
    lanes = [jnp.broadcast_to(index[g : g + 1, :] % TILE, (8, TILE)) for g in range(groups)]

    def pick(t, found):
        at = pl.ds(pl.multiple_of(t * TILE, TILE), TILE)
        news = []
        for half in range(halves):
            heights = prior[0, pl.ds(half * 8, 8), at]
            for g in range(groups):
                picked = jnp.take_along_axis(heights, lanes[g], axis=1)
                news.append(jnp.where(tiles[g] == t, picked, found[half * groups + g]))
        return tuple(news)

    inside = columns // TILE - 2

    def pick_some(k, found):
        for j in range(PICKS):
            found = pick(1 + k * PICKS + j, found)
        return found

    found = (jnp.zeros((8, TILE), jnp.float32),) * (groups * halves)
    found = lax.fori_loop(0, inside // PICKS, pick_some, found)

    for copy in halos:
        copy.wait()
    outer = [factors_of(halo_raw[0, side], halo_raw[1, side]) for side in range(2)]
    sweep_ends(fields_in, halo_in, prior, STEPS_BEFORE, outer)
    found = pick(0, found)
    found = pick(columns // TILE - 1, found)
    for half in range(halves):
        for g in range(groups):
            rows = pl.ds(pl.multiple_of(me * members + half * 8, 8), 8)
            observed[rows, pl.ds(g * TILE, TILE)] = found[half * groups + g]

    def obs_copy(r):
        return pltpu.make_async_remote_copy(
            observed.at[own, :], observed.at[own, :], obs_send.at[r], obs_recv.at[r],
            device_id={"mem": (me + r) % peers}, device_id_type=MESH,
        )

    each(obs_copy, lambda copy: copy.start())
    for q in (0, 2, 3):
        each(functools.partial(in_copy, q), lambda copy: copy.start())
    grid[:, own, :] = prior[:, :, pl.ds(pl.multiple_of(me * width, width), width)]
    each(obs_copy, lambda copy: copy.wait())

    predicted = observed[...]
    spread = predicted - jnp.sum(predicted, axis=0, keepdims=True) * (1.0 / count)
    innovation = value[...] + noise[...] - predicted
    scaled = spread / variance[...]
    rows_id = lax.broadcasted_iota(jnp.int32, (count, count), 0)
    cols_id = lax.broadcasted_iota(jnp.int32, (count, count), 1)
    unit = jnp.where(rows_id == cols_id, 1.0, 0.0).astype(jnp.float32)
    low = float(count - 1)
    inner = dot(scaled, spread, ((1,), (1,))) + low * unit
    update = dot(innovation, scaled, ((1,), (1,)))
    widest = jnp.max(jnp.sum(jnp.abs(inner), axis=0, keepdims=True), axis=1, keepdims=True)
    total = jnp.sum(jnp.sum(inner * unit, axis=0, keepdims=True), axis=1, keepdims=True)
    high = jnp.minimum(widest, total)
    rate = 2.0 / (high + low)
    gap = 2.0 * low / (high + low)
    remainder = unit - rate * inner
    inverse = rate * unit
    for n in range(SQUARINGS):
        multiply = dot if n < EXACT else dot3
        shrink = gap * (2.0 - gap)
        scale = 2.0 / (1.0 + shrink)
        gap = scale * shrink
        if n == 0:
            inverse = (scale * rate) * (unit + remainder)
            square = multiply(remainder, remainder)
        else:
            both = multiply(jnp.concatenate([remainder, inverse], axis=0), remainder)
            square, inverse = both[:count], scale * (inverse + both[count:])
        remainder = scale * square + (1.0 - scale) * unit
    inverse = inverse + dot3(inverse, remainder)
    first_try = dot3(update, inverse)
    update = first_try + dot3(update - dot(first_try, inner), inverse)

    def out_copy(q, r):
        peer = (me + r) % peers
        t = part_of(me, q)
        return pltpu.make_async_remote_copy(
            mixed.at[:, pl.ds(pl.multiple_of(peer * members, members), members), pl.ds(pl.multiple_of(t * TILE, TILE), TILE)],
            analysed.at[:, :, pl.ds(pl.multiple_of(me * width + t * TILE, TILE), TILE)],
            out_send.at[q, r], out_recv.at[q, r], device_id={"mem": peer}, device_id_type=MESH,
        )

    for q in range(parts):
        each(functools.partial(in_copy, q), lambda copy: copy.wait())
        at = pl.ds(pl.multiple_of(part_of(me, q) * TILE, TILE), TILE)
        block = jnp.concatenate([grid[f, :, at] for f in range(3)], axis=1)
        block = block + dot3(update, block)
        for f in range(3):
            mixed[f, :, at] = block[:, f * TILE : (f + 1) * TILE]
        each(functools.partial(out_copy, q), lambda copy: copy.start())
    analysed[:, :, pl.ds(pl.multiple_of(me * width, width), width)] = mixed[:, own, :]
    each(functools.partial(out_copy, 0), lambda copy: copy.wait())
    edges = to_neighbours(analysed, halo_out, edge_send, edge_recv)
    for copy in edges:
        copy.start()
    for q in range(1, parts):
        each(functools.partial(out_copy, q), lambda copy: copy.wait())
    sweep_all(analysed, out, STEPS_AFTER, lambda k: None)
    for copy in edges:
        copy.wait()
    sweep_ends(analysed, halo_out, out, STEPS_AFTER, outer)


def local(state, courant, angle, obs_index, obs_value, obs_variance, perturb):
    members, fields, columns = state.shape
    nobs = obs_index.shape[0]
    peers = lax.axis_size("mem")
    count, width = peers * members, columns // peers
    parts = width // TILE
    f32 = jnp.float32
    dma = pltpu.SemaphoreType.DMA
    result = pl.pallas_call(
        kernel,
        out_shape=pltpu.VMEM((fields, members, columns), f32),
        in_specs=[pl.BlockSpec(memory_space=pltpu.HBM)] * 7,
        out_specs=pl.BlockSpec(memory_space=pltpu.VMEM),
        scratch_shapes=[
            pltpu.VMEM((fields, members, columns), f32),
            pltpu.VMEM((2, 1, columns), f32),
            pltpu.VMEM((3, 8, columns), f32),
            pltpu.VMEM((nobs // TILE, TILE), jnp.int32),
            pltpu.VMEM((1, nobs), f32),
            pltpu.VMEM((1, nobs), f32),
            pltpu.VMEM((count, nobs), f32),
            pltpu.VMEM((fields, members, columns), f32),
            pltpu.VMEM((count, nobs), f32),
            pltpu.VMEM((fields, count, width), f32),
            pltpu.VMEM((fields, count, width), f32),
            pltpu.VMEM((fields, members, columns), f32),
            pltpu.VMEM((2, fields, members, TILE), f32),
            pltpu.VMEM((2, 2, 1, TILE), f32),
            pltpu.VMEM((2, fields, members, TILE), f32),
            dma((6,)), dma((columns // CHUNK,)), dma((3, 2)), dma((3, 2)), dma((peers,)), dma((peers,)),
            dma((parts, peers)), dma((parts, peers)), dma((parts, peers)), dma((parts, peers)), dma((2,)), dma((2,)),
        ],
        compiler_params=pltpu.CompilerParams(collective_id=0, has_side_effects=True, vmem_limit_bytes=60 * 2**20),
    )(
        jnp.transpose(state, (1, 0, 2)), courant[None, :], angle[None, :],
        obs_index.reshape(nobs // TILE, TILE), obs_value[None, :], obs_variance[None, :], perturb,
    )
    return jnp.transpose(result, (1, 0, 2))


def solution(mesh):
    in_specs = (
        P("mem", None, "strip"),
        P("strip"),
        P("strip"),
        P("strip"),
        P("strip"),
        P("strip"),
        P(None, "strip"),
    )
    out_specs = P("mem", None, "strip")
    return jax.shard_map(local, mesh=mesh, in_specs=in_specs, out_specs=out_specs, check_vma=False)
```

time: 78.4 us -> 60.8 us (0.78)
  Pallas kernels: 70.9 us -> 59.6 us
  local copies, waits for them, and re-layouts: 7.15 us -> 1.15 us
    pallas_call x1, Pallas kernels: 70.9 us -> 59.6 us  [local(): pl.pallas_call(kernel, out_shape=pltpu.VMEM((fields, members, columns), f...]
    unnamed x15 -> x1, local copies, waits for them, and re-layouts: 7.15 us -> 1.15 us
where the time goes in v1:
time: 60.8 us; the launch traced here: 60.7 us
  Pallas kernels  59.6 us (98%)
  local copies, waits for them, and re-layouts  1.15 us (2%)
    pallas_call x1, Pallas kernels, local(): pl.pallas_call(kernel, out_shape=pltpu.VMEM((fields, members, columns), f...  59.6 us

profile of v1, /device:TPU:1, one launch (start us, length us, event | category | flops | bytes accessed | tf_op | source)
XLA Modules:
  0.0 60.7 jit_solution(9336340122418899959)
XLA Ops:
  0.0 59.6 %shard_map.73 = f32[3,16,8192]{2,1,0:T(8,128)S(1)} custom-call(f32[3,16,8192]{2,1,0:T(8,128)} %bitcast.8, f32[1,8192]{1,0:T(1,128)} %bitcast.9, f32[1,8192]{1,0:T(1,128)} %bitcast.10, s32[4,128]{1,0:T(4,128)} %bitcast.11, f32[1,512]{1,0:T(1,128)} %bitcast.12, f32[1,512]{1,0:T(1,128)} %bitcast.13, f32[256,512]{1,0:T(8,128)} %perturb.1), custom_call_target="tpu_custom_call" | custom-call | tf_op jit(solution)/shard_map/pallas_call | solution.py:328
  59.6 1.1 %copy.9 = f32[16,3,8192]{2,0,1:T(8,128)} copy(f32[16,3,8192]{2,0,1:T(8,128)S(1)} %bitcast.7) | data formatting | bytes 3145728

commit v2 on v1

--- a/solution.py
+++ b/solution.py
@@ -10,10 +10,10 @@
 STEPS_BEFORE = 4
 STEPS_AFTER = 2
 SQUARINGS = 12
-EXACT = 5
+EXACT = 4
+ROUGH = 2
 CHUNK = 1024
 TILE = 128
-PICKS = 31
 MESH = pl.DeviceIdType.MESH
 HIGH = lax.Precision.HIGHEST
 
@@ -22,13 +22,20 @@
     return lax.dot_general(a, b, (dims, ((), ())), precision=HIGH, preferred_element_type=jnp.float32)
 
 
-def dot3(a, b):
+def dot3(a, b, dims=((1,), (0,))):
+    def one(x, y):
+        return lax.dot_general(x, y, (dims, ((), ())), preferred_element_type=jnp.float32)
+
     a_hi, b_hi = a.astype(jnp.bfloat16), b.astype(jnp.bfloat16)
     a_lo = (a - a_hi.astype(jnp.float32)).astype(jnp.bfloat16)
     b_lo = (b - b_hi.astype(jnp.float32)).astype(jnp.bfloat16)
     rows = a.shape[0]
-    both = jnp.dot(jnp.concatenate([a_hi, a_lo], axis=0), b_hi, preferred_element_type=jnp.float32)
-    return both[:rows] + (both[rows:] + jnp.dot(a_hi, b_lo, preferred_element_type=jnp.float32))
+    both = one(jnp.concatenate([a_hi, a_lo], axis=0), b_hi)
+    return both[:rows] + (both[rows:] + one(a_hi, b_lo))
+
+
+def dot1(a, b):
+    return jnp.dot(a.astype(jnp.bfloat16), b.astype(jnp.bfloat16), preferred_element_type=jnp.float32)
 
 
 def cosine_sine(angle):
@@ -95,7 +102,8 @@
 
     def state_load(k):
         at = pl.ds(k * CHUNK, CHUNK)
-        return pltpu.make_async_copy(state.at[:, :, at], fields_in.at[:, :, at], state_sem.at[k])
+        to = pl.ds(TILE + k * CHUNK, CHUNK)
+        return pltpu.make_async_copy(state.at[:, :, at], fields_in.at[:, :, to], state_sem.at[k])
 
     for load in loads[:2]:
         load.start()
@@ -133,37 +141,25 @@
 
     def coefficients(k, carry):
         at = pl.ds(pl.multiple_of(k * CHUNK, CHUNK), CHUNK)
+        to = pl.ds(pl.multiple_of(TILE + k * CHUNK, TILE), CHUNK)
         for f, factor in enumerate(factors_of(raw[0, :, at], raw[1, :, at])):
-            coef[f, :, at] = factor
+            coef[f, :, to] = factor
         return carry
 
     lax.fori_loop(0, chunks, coefficients, 0)
 
-    def sweep(source, target, steps, k, before=TILE, after=TILE):
-        window = pl.ds(pl.multiple_of(k * CHUNK - before, TILE), CHUNK + before + after)
+    def sweep(source, target, steps, k):
+        window = pl.ds(pl.multiple_of(k * CHUNK, TILE), CHUNK + 2 * TILE)
         to = pl.ds(pl.multiple_of(k * CHUNK, CHUNK), CHUNK)
         factors = [coef[f, :, window] for f in range(3)]
         for half in range(halves):
             rows = pl.ds(half * 8, 8)
             news = advance([source[f, rows, window] for f in range(3)], factors, steps)
             for f in range(3):
-                target[f, rows, to] = news[f][:, before : before + CHUNK]
-
-    def sweep_all(source, target, steps, ready):
-        ready(0)
-        ready(1)
-        sweep(source, target, steps, 0, before=0)
-
-        def body(k, carry):
-            ready(k + 1)
-            sweep(source, target, steps, k)
-            return carry
-
-        lax.fori_loop(1, chunks - 1, body, 0)
-        sweep(source, target, steps, chunks - 1, after=0)
+                target[f, rows, to] = news[f][:, TILE : TILE + CHUNK]
 
     def sweep_ends(source, halo, target, steps, outer):
-        two = [pl.ds(columns - 2 * TILE, 2 * TILE), pl.ds(0, 2 * TILE)]
+        two = [pl.ds(columns - TILE, 2 * TILE), pl.ds(TILE, 2 * TILE)]
         for side in range(2):
             inner = two[1 - side]
 
@@ -178,11 +174,8 @@
                 for f in range(3):
                     target[f, rows, (first, last)[side]] = news[f][:, TILE : 2 * TILE]
 
-    def state_ready(k):
-        at = pl.ds(pl.multiple_of(k * CHUNK, CHUNK), CHUNK)
-        pltpu.make_async_copy(state.at[:, :, at], fields_in.at[:, :, at], state_sem.at[k]).wait()
-
-    sweep_all(fields_in, prior, STEPS_BEFORE, state_ready)
+    for k in range(chunks):
+        state_load(k).wait()
 
     def part_of(peer, q):
         return q + (peer // (peers - 1)) * (parts - 1 - 2 * q)
@@ -202,8 +195,6 @@
             return carry
 
         lax.fori_loop(1, peers, body, 0)
-
-    each(functools.partial(in_copy, 1), lambda copy: copy.start())
 
     for load in loads[2:]:
         load.wait()
@@ -221,15 +212,24 @@
                 news.append(jnp.where(tiles[g] == t, picked, found[half * groups + g]))
         return tuple(news)
 
-    inside = columns // TILE - 2
-
-    def pick_some(k, found):
-        for j in range(PICKS):
-            found = pick(1 + k * PICKS + j, found)
+    blocks = CHUNK // width
+
+    def step_and_send(i, found):
+        k = (me // blocks + 1 + i) % chunks
+        sweep(fields_in, prior, STEPS_BEFORE, k)
+        for j in range(CHUNK // TILE):
+            found = pick(k * (CHUNK // TILE) + j, found)
+        for j in range(blocks):
+            peer = k * blocks + j
+
+            @pl.when(peer != me)
+            def _(peer=peer):
+                in_copy(1, (peer + peers - me) % peers).start()
+
         return found
 
     found = (jnp.zeros((8, TILE), jnp.float32),) * (groups * halves)
-    found = lax.fori_loop(0, inside // PICKS, pick_some, found)
+    found = lax.fori_loop(0, chunks, step_and_send, found)
 
     for copy in halos:
         copy.wait()
@@ -242,22 +242,40 @@
             rows = pl.ds(pl.multiple_of(me * members + half * 8, 8), 8)
             observed[rows, pl.ds(g * TILE, TILE)] = found[half * groups + g]
 
+    chips = peers // 2
+    sibling = me + 1 - 2 * (me % 2)
+
     def obs_copy(r):
         return pltpu.make_async_remote_copy(
             observed.at[own, :], observed.at[own, :], obs_send.at[r], obs_recv.at[r],
-            device_id={"mem": (me + r) % peers}, device_id_type=MESH,
+            device_id={"mem": (me + 2 * r) % peers}, device_id_type=MESH,
         )
 
-    each(obs_copy, lambda copy: copy.start())
+    def obs_share(r):
+        rows = pl.ds(pl.multiple_of((me + peers - 2 * r) % peers * members, members), members)
+        return pltpu.make_async_remote_copy(
+            observed.at[rows, :], observed.at[rows, :], obs_send.at[chips + r], obs_recv.at[chips + r],
+            device_id={"mem": sibling}, device_id_type=MESH,
+        )
+
+    for r in range(1, chips):
+        obs_copy(r).start()
+    obs_share(0).start()
     for q in (0, 2, 3):
         each(functools.partial(in_copy, q), lambda copy: copy.start())
     grid[:, own, :] = prior[:, :, pl.ds(pl.multiple_of(me * width, width), width)]
-    each(obs_copy, lambda copy: copy.wait())
+    for r in range(1, chips):
+        obs_copy(r).wait_recv()
+        obs_share(r).start()
+    for r in range(chips):
+        obs_share(r).wait()
+    for r in range(1, chips):
+        obs_copy(r).wait_send()
 
     predicted = observed[...]
     spread = predicted - jnp.sum(predicted, axis=0, keepdims=True) * (1.0 / count)
     innovation = value[...] + noise[...] - predicted
-    scaled = spread / variance[...]
+    scaled = spread * (1.0 / variance[...])
     rows_id = lax.broadcasted_iota(jnp.int32, (count, count), 0)
     cols_id = lax.broadcasted_iota(jnp.int32, (count, count), 1)
     unit = jnp.where(rows_id == cols_id, 1.0, 0.0).astype(jnp.float32)
@@ -272,7 +290,7 @@
     remainder = unit - rate * inner
     inverse = rate * unit
     for n in range(SQUARINGS):
-        multiply = dot if n < EXACT else dot3
+        multiply = dot if n < EXACT else dot3 if n < SQUARINGS - ROUGH else dot1
         shrink = gap * (2.0 - gap)
         scale = 2.0 / (1.0 + shrink)
         gap = scale * shrink
@@ -283,8 +301,8 @@
             both = multiply(jnp.concatenate([remainder, inverse], axis=0), remainder)
             square, inverse = both[:count], scale * (inverse + both[count:])
         remainder = scale * square + (1.0 - scale) * unit
-    inverse = inverse + dot3(inverse, remainder)
-    first_try = dot3(update, inverse)
+    inverse = inverse + dot1(inverse, remainder)
+    first_try = dot(update, inverse)
     update = first_try + dot3(update - dot(first_try, inner), inverse)
 
     def out_copy(q, r):
@@ -292,7 +310,7 @@
         t = part_of(me, q)
         return pltpu.make_async_remote_copy(
             mixed.at[:, pl.ds(pl.multiple_of(peer * members, members), members), pl.ds(pl.multiple_of(t * TILE, TILE), TILE)],
-            analysed.at[:, :, pl.ds(pl.multiple_of(me * width + t * TILE, TILE), TILE)],
+            analysed.at[:, :, pl.ds(pl.multiple_of(TILE + me * width + t * TILE, TILE), TILE)],
             out_send.at[q, r], out_recv.at[q, r], device_id={"mem": peer}, device_id_type=MESH,
         )
 
@@ -304,14 +322,19 @@
         for f in range(3):
             mixed[f, :, at] = block[:, f * TILE : (f + 1) * TILE]
         each(functools.partial(out_copy, q), lambda copy: copy.start())
-    analysed[:, :, pl.ds(pl.multiple_of(me * width, width), width)] = mixed[:, own, :]
+    analysed[:, :, pl.ds(pl.multiple_of(TILE + me * width, TILE), width)] = mixed[:, own, :]
     each(functools.partial(out_copy, 0), lambda copy: copy.wait())
-    edges = to_neighbours(analysed, halo_out, edge_send, edge_recv)
+    edges = to_neighbours(analysed.at[:, :, pl.ds(TILE, columns)], halo_out, edge_send, edge_recv)
     for copy in edges:
         copy.start()
     for q in range(1, parts):
         each(functools.partial(out_copy, q), lambda copy: copy.wait())
-    sweep_all(analysed, out, STEPS_AFTER, lambda k: None)
+
+    def last_steps(k, carry):
+        sweep(analysed, out, STEPS_AFTER, k)
+        return carry
+
+    lax.fori_loop(0, chunks, last_steps, 0)
     for copy in edges:
         copy.wait()
     sweep_ends(analysed, halo_out, out, STEPS_AFTER, outer)
@@ -322,7 +345,7 @@
     nobs = obs_index.shape[0]
     peers = lax.axis_size("mem")
     count, width = peers * members, columns // peers
-    parts = width // TILE
+    parts, wide = width // TILE, columns + 2 * TILE
     f32 = jnp.float32
     dma = pltpu.SemaphoreType.DMA
     result = pl.pallas_call(
@@ -331,9 +354,9 @@
         in_specs=[pl.BlockSpec(memory_space=pltpu.HBM)] * 7,
         out_specs=pl.BlockSpec(memory_space=pltpu.VMEM),
         scratch_shapes=[
-            pltpu.VMEM((fields, members, columns), f32),
+            pltpu.VMEM((fields, members, wide), f32),
             pltpu.VMEM((2, 1, columns), f32),
-            pltpu.VMEM((3, 8, columns), f32),
+            pltpu.VMEM((3, 8, wide), f32),
             pltpu.VMEM((nobs // TILE, TILE), jnp.int32),
             pltpu.VMEM((1, nobs), f32),
             pltpu.VMEM((1, nobs), f32),
@@ -342,7 +365,7 @@
             pltpu.VMEM((count, nobs), f32),
             pltpu.VMEM((fields, count, width), f32),
             pltpu.VMEM((fields, count, width), f32),
-            pltpu.VMEM((fields, members, columns), f32),
+            pltpu.VMEM((fields, members, wide), f32),
             pltpu.VMEM((2, fields, members, TILE), f32),
             pltpu.VMEM((2, 2, 1, TILE), f32),
             pltpu.VMEM((2, fields, members, TILE), f32),

time: 60.8 us -> 58 us (0.954)
  Pallas kernels: 59.6 us -> 56.8 us
    pallas_call x1, Pallas kernels: 59.6 us -> 56.8 us  [local(): pl.pallas_call(kernel, out_shape=pltpu.VMEM((fields, members, columns), f...]
where the time goes in v2:
time: 58 us; the launch traced here: 57.9 us
  Pallas kernels  56.8 us (98%)
  local copies, waits for them, and re-layouts  1.15 us (2%)
    pallas_call x1, Pallas kernels, local(): pl.pallas_call(kernel, out_shape=pltpu.VMEM((fields, members, columns), f...  56.8 us

profile of v2, /device:TPU:1, one launch (start us, length us, event | category | flops | bytes accessed | tf_op | source)
XLA Modules:
  0.0 57.9 jit_solution(7101215326544196881)
XLA Ops:
  0.0 56.8 %shard_map.73 = f32[3,16,8192]{2,1,0:T(8,128)S(1)} custom-call(f32[3,16,8192]{2,1,0:T(8,128)} %bitcast.8, f32[1,8192]{1,0:T(1,128)} %bitcast.9, f32[1,8192]{1,0:T(1,128)} %bitcast.10, s32[4,128]{1,0:T(4,128)} %bitcast.11, f32[1,512]{1,0:T(1,128)} %bitcast.12, f32[1,512]{1,0:T(1,128)} %bitcast.13, f32[256,512]{1,0:T(8,128)} %perturb.1), custom_call_target="tpu_custom_call" | custom-call | tf_op jit(solution)/shard_map/pallas_call | solution.py:351
  56.8 1.1 %copy.9 = f32[16,3,8192]{2,0,1:T(8,128)} copy(f32[16,3,8192]{2,0,1:T(8,128)S(1)} %bitcast.7) | data formatting | bytes 3145728

commit v3 on v2

--- a/solution.py
+++ b/solution.py
@@ -49,13 +49,14 @@
     h, u, v = fields
     c, cosine, sine = coefs
     last = h.shape[-1] - 1
+    half = 0.5 * c
     for _ in range(steps):
         a = u + h
         b = u - h
-        a = a - c * (a - pltpu.roll(a, 1, axis=1))
-        b = b + c * (pltpu.roll(b, last, axis=1) - b)
-        speed = 0.5 * (a + b)
-        h = 0.5 * (a - b)
+        da = a - pltpu.roll(a, 1, axis=1)
+        db = pltpu.roll(b, last, axis=1) - b
+        speed = u + half * (db - da)
+        h = h - half * (da + db)
         u = cosine * speed + sine * v
         v = cosine * v - sine * speed
     return h, u, v

time: 58 us -> 58 us (level)
  no operation moved by 1% of the time
where the time goes in v3:
time: 58 us; the launch traced here: 57.9 us
  Pallas kernels  56.7 us (98%)
  local copies, waits for them, and re-layouts  1.15 us (2%)
    pallas_call x1, Pallas kernels, local(): pl.pallas_call(kernel, out_shape=pltpu.VMEM((fields, members, columns), f...  56.7 us

profile of v3, /device:TPU:1, one launch (start us, length us, event | category | flops | bytes accessed | tf_op | source)
XLA Modules:
  0.0 57.9 jit_solution(11705133107013271554)
XLA Ops:
  0.0 56.7 %shard_map.73 = f32[3,16,8192]{2,1,0:T(8,128)S(1)} custom-call(f32[3,16,8192]{2,1,0:T(8,128)} %bitcast.8, f32[1,8192]{1,0:T(1,128)} %bitcast.9, f32[1,8192]{1,0:T(1,128)} %bitcast.10, s32[4,128]{1,0:T(4,128)} %bitcast.11, f32[1,512]{1,0:T(1,128)} %bitcast.12, f32[1,512]{1,0:T(1,128)} %bitcast.13, f32[256,512]{1,0:T(8,128)} %perturb.1), custom_call_target="tpu_custom_call" | custom-call | tf_op jit(solution)/shard_map/pallas_call | solution.py:352
  56.8 1.1 %copy.9 = f32[16,3,8192]{2,0,1:T(8,128)} copy(f32[16,3,8192]{2,0,1:T(8,128)S(1)} %bitcast.7) | data formatting | bytes 3145728
